TPU v7x, 512 devices: a whole 4x8x8 slice. The times are simulated.
512 devices in a mesh: frame: 16 (over z, core), tok: 32 (over y, x).
Axes of the slice: x: 4, y: 8, z: 8, core: 2. Of those that a mesh axis runs over, the one named last changes fastest.
Arguments:
- latents: bfloat16 [64, 1024, 3072], P('frame', 'tok'), may hold values from -3 to 3
- queries: bfloat16 [64, 1024, 3072], P('frame', 'tok')
- keys: bfloat16 [64, 1024, 3072], P('frame', 'tok')
- values: bfloat16 [64, 1024, 3072], P('frame', 'tok'), may hold values from -48 to 48
- levels: int32 [64], P('frame'), may hold values from 0 to 127, as said below
- reach: int32 [64], P('frame'), may hold values from 0 to 2, as said below
- gates: bfloat16 [128, 3072], P('frame'), may hold values from 0.099609375 to 1.8984375
- steps_table: float32 [128], P('frame'), may hold values from 0.25 to 1
- fresh: bfloat16 [1024, 3072], P('tok'), may hold values from -6 to 6
Outputs:
- updated: bfloat16 [64, 1024, 3072], P('frame', 'tok')
- next_queue: bfloat16 [64, 1024, 3072], P('frame', 'tok')
Inputs may be any that keep to these rules, and one draw needn't show every extreme that they name: Frame f's level is 2 f or 2 f + 1, so levels rise along the queue by 1, 2 or 3; frame 0 has level 0 and the last frame level 127. `reach`: the last frame's window is exactly 2.
All inputs are finite; a program needn't handle non-finite values.
Results may differ from a plain program's by a relative error of at most 0.0036.
Values may be sent and summed in bfloat16 or wider, within the bound.
A program may use at most 64 MiB of HBM per device.

v0:
```python
import jax
import jax.numpy as jnp
from jax import lax
from jax.sharding import PartitionSpec as P

HEADS = 24
HEAD_DIM = 128
REACH = 2


masked_score = -1e30


def from_behind(value, axis, steps):
    count = lax.axis_size(axis)
    leading, last = (max(0, -steps), min(count, count - steps))
    return lax.ppermute(value, axis, [(source, source + steps) for source in range(leading, last)])


def split_heads(block_rows):
    frames, rows, width = block_rows.shape
    shaped = block_rows.reshape(frames, rows, HEADS, HEAD_DIM).transpose(0, 2, 1, 3)
    return shaped.reshape(frames * HEADS, rows, HEAD_DIM)


def per_device(latents, queries, keys, values, levels, reach, gates, steps_table, fresh):
    group_frames, shard_tokens, width = latents.shape
    token_devices = lax.axis_size("tok")
    per_frame = token_devices // group_frames
    position = lax.axis_index("tok")
    group_index = lax.axis_index("frame")
    slot = position // per_frame
    frame_index = group_index * group_frames + slot
    query_heads, key_heads, value_heads = (
        lax.all_to_all(split_heads(queries), "tok", split_axis=0, concat_axis=1, tiled=True),
        lax.all_to_all(split_heads(keys), "tok", split_axis=0, concat_axis=1, tiled=True),
        lax.all_to_all(split_heads(values), "tok", split_axis=0, concat_axis=1, tiled=True),
    )
    pair = jnp.stack([key_heads, value_heads], 0)
    windows = [pair]
    moving = pair
    for step in range(REACH):
        moving = from_behind(moving, ("frame", "tok"), per_frame)
        windows = [moving] + windows
    heads_here, frame_len, head_dim = query_heads.shape
    window = jnp.stack(windows, 2).reshape(2, heads_here, (REACH + 1) * frame_len, head_dim)
    slots = jnp.arange(group_frames, dtype=jnp.int32)
    reach_frame = jnp.sum(jnp.where(slots == slot, reach, 0))
    key_frames = frame_index - REACH + jnp.arange(REACH + 1, dtype=jnp.int32)
    slot_ok = (key_frames >= 0) & (key_frames >= frame_index - reach_frame)
    column_ok = jnp.repeat(slot_ok, frame_len)
    block = min(512, frame_len)
    blocks = frame_len // block
    query_blocks = query_heads.reshape(heads_here * blocks, block, head_dim)
    scale = 1.0 / HEAD_DIM**0.5

    def one_block(item):
        head = item // blocks
        query_rows = lax.dynamic_index_in_dim(query_blocks, item, 0, keepdims=False)
        key_rows = lax.dynamic_index_in_dim(window[0], head, 0, keepdims=False)
        value_rows = lax.dynamic_index_in_dim(window[1], head, 0, keepdims=False)
        scores = (
            lax.dot_general(
                query_rows, key_rows, (((1,), (1,)), ((), ())), preferred_element_type=jnp.float32
            )
            * scale
        )
        scores = jnp.where(column_ok[None, :], scores, masked_score)
        top_score = jnp.max(scores, axis=1, keepdims=True)
        weights = jnp.exp(scores - top_score)
        running_sum = jnp.sum(weights, axis=1, keepdims=True)
        numerator = jnp.dot(
            weights.astype(jnp.bfloat16), value_rows, preferred_element_type=jnp.float32
        )
        return (numerator / running_sum).astype(jnp.bfloat16)

    attn_heads = lax.map(one_block, jnp.arange(heads_here * blocks, dtype=jnp.int32))
    attn_heads = attn_heads.reshape(heads_here, frame_len, head_dim)
    returned = lax.all_to_all(attn_heads, "tok", split_axis=1, concat_axis=0, tiled=True)
    attn = returned.reshape(group_frames, HEADS, shard_tokens, head_dim).transpose(0, 2, 1, 3)
    attn = attn.reshape(group_frames, shard_tokens, width)
    level_rows = gates.shape[0]
    local_levels = levels - group_index * level_rows
    one_hot = local_levels[:, None] == jnp.arange(level_rows, dtype=jnp.int32)[None, :]
    gate_rows = jnp.dot(one_hot.astype(jnp.bfloat16), gates, preferred_element_type=jnp.float32)
    step_sizes = jnp.sum(one_hot.astype(jnp.float32) * steps_table[None, :], axis=1)
    updated = latents.astype(jnp.float32) - step_sizes[:, None, None] * gate_rows[
        :, None, :
    ] * attn.astype(jnp.float32)
    updated = updated.astype(jnp.bfloat16)
    incoming = from_behind(updated[0:1], "frame", -1)
    is_last = group_index == lax.axis_size("frame") - 1
    incoming = jnp.where(is_last, fresh[None], incoming)
    next_queue = jnp.concatenate([updated[1:], incoming], 0)
    return (updated, next_queue)


def solution(mesh):
    in_specs = (
        P("frame", "tok", None),
        P("frame", "tok", None),
        P("frame", "tok", None),
        P("frame", "tok", None),
        P("frame"),
        P("frame"),
        P("frame", None),
        P("frame"),
        P("tok", None),
    )
    out_specs = (P("frame", "tok", None), P("frame", "tok", None))
    return jax.shard_map(
        per_device, mesh=mesh, in_specs=in_specs, out_specs=out_specs, check_vma=False
    )
```

profile of v0, /device:TPU:1, one launch (start us, length us, event | category | flops | bytes accessed | tf_op | source)
XLA Modules:
  0.0 347.2 jit_solution(6486500174593469258)
XLA Ops:
  0.7 1.4 copy.67
  2.1 1.0 copy.57
  3.1 10.5 %all-to-all-start.2 = ((bf16[96,32,128]{2,1,0:T(8,128)(2,1)}), bf16[96,32,128]{2,1,0:T(8,128)(2,1)S(1)}, u32[]{:S(2)}, u32[]{:S(2)}) async-start(bf16[96,32,128]{2,1,0:T(8,128)(2,1)} %bitcast.11), calls=%async_computation.2 | async-start | bytes 1572864 | tf_op jit(solution)/shard_map/all_to_all | solution.py:37
  13.9 1.0 copy.55
  14.9 19.8 %all-to-all-done.2 = bf16[96,32,128]{2,1,0:T(8,128)(2,1)S(1)} async-done(((bf16[96,32,128]{2,1,0:T(8,128)(2,1)}), bf16[96,32,128]{2,1,0:T(8,128)(2,1)S(1)}, u32[]{:S(2)}, u32[]{:S(2)}) %all-to-all-start.2) | async-done | bytes 786464 | tf_op jit(solution)/shard_map/all_to_all | solution.py:37
  34.7 5.8 %all-to-all-start.1 = ((bf16[96,32,128]{2,1,0:T(8,128)(2,1)}), bf16[96,32,128]{2,1,0:T(8,128)(2,1)S(1)}, u32[]{:S(2)}, u32[]{:S(2)}) async-start(bf16[96,32,128]{2,1,0:T(8,128)(2,1)} %bitcast.6), calls=%async_computation.1 | async-start | bytes 1572864 | tf_op jit(solution)/shard_map/all_to_all | solution.py:36
  40.5 19.7 %all-to-all-done.1 = bf16[96,32,128]{2,1,0:T(8,128)(2,1)S(1)} async-done(((bf16[96,32,128]{2,1,0:T(8,128)(2,1)}), bf16[96,32,128]{2,1,0:T(8,128)(2,1)S(1)}, u32[]{:S(2)}, u32[]{:S(2)}) %all-to-all-start.1) | async-done | bytes 786464 | tf_op jit(solution)/shard_map/all_to_all | solution.py:36
  60.5 3.9 %collective-permute-start = (bf16[2,3,1024,128]{3,2,1,0:T(8,128)(2,1)S(1)}, bf16[2,3,1024,128]{3,2,1,0:T(8,128)(2,1)}, u32[]{:S(2)}, u32[]{:S(2)}) collective-permute-start(bf16[2,3,1024,128]{3,2,1,0:T(8,128)(2,1)S(1)} %get-tuple-element.112), channel_id=1, source_target_pairs={{0,8},{1,9},{2,10},{3,11},{4,12},{5,13},{6,14},{7,15},{8,16},{9,17... | collective-permute-start | bytes 4718600 | tf_op jit(solution)/shard_map/ppermute | solution.py:17
  64.6 66.8 %collective-permute-done = bf16[2,3,1024,128]{3,2,1,0:T(8,128)(2,1)} collective-permute-done((bf16[2,3,1024,128]{3,2,1,0:T(8,128)(2,1)S(1)}, bf16[2,3,1024,128]{3,2,1,0:T(8,128)(2,1)}, u32[]{:S(2)}, u32[]{:S(2)}) %collective-permute-start) | collective-permute-done | bytes 1572896 | tf_op jit(solution)/shard_map/ppermute | solution.py:17
  131.4 2.7 collective-permute-start.1
  134.3 1.0 copy.53
  135.3 45.0 %all-to-all-start = ((bf16[96,32,128]{2,1,0:T(8,128)(2,1)}), bf16[96,32,128]{2,1,0:T(8,128)(2,1)S(1)}, u32[]{:S(2)}, u32[]{:S(2)}) async-start(bf16[96,32,128]{2,1,0:T(8,128)(2,1)} %bitcast.1), calls=%async_computation | async-start | bytes 1572864 | tf_op jit(solution)/shard_map/all_to_all | solution.py:35
  180.3 0.6 fusion.34
  181.6 43.1 %all-to-all-done = bf16[96,32,128]{2,1,0:T(8,128)(2,1)S(1)} async-done(((bf16[96,32,128]{2,1,0:T(8,128)(2,1)}), bf16[96,32,128]{2,1,0:T(8,128)(2,1)S(1)}, u32[]{:S(2)}, u32[]{:S(2)}) %all-to-all-start) | async-done | bytes 786464 | tf_op jit(solution)/shard_map/all_to_all | solution.py:35
  224.8 2.1 pad_maximum_fusion
  226.9 2.4 copy.59
  229.4 67.9 %while.13 = (s32[]{:T(128)}, bf16[6,512,128]{2,1,0:T(8,128)(2,1)S(1)}, s32[6]{0:T(128)S(1)}, bf16[6,512,128]{2,1,0:T(8,128)(2,1)S(1)}, bf16[2,3,3072,128]{3,2,1,...) while((s32[]{:T(128)}, ...), condition=%wide.region_5.6_spmd.clone, body=%wide.region_2.5_spmd.clone.sunk | while | flops 822737920 | bytes 30175580 | solution.py:77
  233.9 2.7 fusion.46
  236.6 1.2 fusion.47
  237.8 1.4 fusion.48
  239.2 1.4 fusion.49
  245.3 2.7 fusion.46
  248.0 1.2 fusion.47
  249.1 1.4 fusion.48
  250.6 1.4 fusion.49
  256.6 2.7 fusion.46
  259.3 1.2 fusion.47
  260.4 1.4 fusion.48
  261.9 1.4 fusion.49
  267.9 2.7 fusion.46
  270.6 1.2 fusion.47
  271.8 1.4 fusion.48
  273.2 1.4 fusion.49
  279.2 2.7 fusion.46
  281.9 1.2 fusion.47
  283.1 1.4 fusion.48
  284.5 1.4 fusion.49
  290.6 2.7 fusion.46
  293.3 1.2 fusion.47
  294.4 1.4 fusion.48
  295.8 1.4 fusion.49
  297.3 1.6 copy.60
  299.0 9.2 %all-to-all-start.3 = ((bf16[3,1024,128]{2,0,1:T(4,128)(2,1)}), bf16[3,1024,128]{2,0,1:T(4,128)(2,1)S(1)}, u32[]{:S(2)}, u32[]{:S(2)}) async-start(bf16[3,1024,128]{2,0,1:T(4,128)(2,1)} %copy.60), calls=%async_computation.3 | async-start | bytes 2097152 | tf_op jit(solution)/shard_map/all_to_all | solution.py:79
  308.6 25.9 %all-to-all-done.3 = bf16[3,1024,128]{2,0,1:T(4,128)(2,1)S(1)} async-done(((bf16[3,1024,128]{2,0,1:T(4,128)(2,1)}), bf16[3,1024,128]{2,0,1:T(4,128)(2,1)S(1)}, u32[]{:S(2)}, u32[]{:S(2)}) %all-to-all-start.3) | async-done | bytes 786464 | tf_op jit(solution)/shard_map/all_to_all | solution.py:79
  334.9 0.8 copy-done.5
  335.9 4.6 %collective-permute-start.2 = (bf16[1,32,3072]{2,1,0:T(8,128)(2,1)S(1)}, bf16[1,32,3072]{2,1,0:T(8,128)(2,1)S(1)}, u32[]{:S(2)}, u32[]{:S(2)}) collective-permute-start(bf16[1,32,3072]{2,1,0:T(8,128)(2,1)S(1)} %slice.23), channel_id=1, source_target_pairs={{32,0},{64,32},{96,64},{128,96},{160,128},{192,160},{224,192},{256... | collective-permute-start | bytes 589832 | tf_op jit(solution)/shard_map/ppermute | solution.py:17
  340.6 5.6 %collective-permute-done.2 = bf16[1,32,3072]{2,1,0:T(8,128)(2,1)S(1)} collective-permute-done((bf16[1,32,3072]{2,1,0:T(8,128)(2,1)S(1)}, bf16[1,32,3072]{2,1,0:T(8,128)(2,1)S(1)}, u32[]{:S(2)}, u32[]{:S(2)}) %collective-permute-start.2) | collective-permute-done | bytes 196640 | tf_op jit(solution)/shard_map/ppermute | solution.py:17
  346.2 0.9 pad_maximum_fusion.2
  (60 shorter events, 6.3 us)
Async XLA Ops:
  0.6 307.7 %copy-start = (bf16[8,3072]{1,0:T(8,128)(2,1)S(1)}, bf16[8,3072]{1,0:T(8,128)(2,1)}, u32[]{:S(2)}) copy-start(bf16[8,3072]{1,0:T(8,128)(2,1)} %param.17) | copy-start | bytes 147460
  0.6 13.0 %copy-start.3 = (bf16[4,32,3072]{2,1,0:T(8,128)(2,1)S(1)}, bf16[4,32,3072]{2,1,0:T(8,128)(2,1)}, u32[]{:S(2)}) copy-start(bf16[4,32,3072]{2,1,0:T(8,128)(2,1)} %param.13) | copy-start | bytes 2359300
  3.1 31.6 %all-to-all-start.2 = ((bf16[96,32,128]{2,1,0:T(8,128)(2,1)}), bf16[96,32,128]{2,1,0:T(8,128)(2,1)S(1)}, u32[]{:S(2)}, u32[]{:S(2)}) async-start(bf16[96,32,128]{2,1,0:T(8,128)(2,1)} %bitcast.11), calls=%async_computation.2 | async-start | bytes 1572864 | tf_op jit(solution)/shard_map/all_to_all | solution.py:37
  34.7 25.5 %all-to-all-start.1 = ((bf16[96,32,128]{2,1,0:T(8,128)(2,1)}), bf16[96,32,128]{2,1,0:T(8,128)(2,1)S(1)}, u32[]{:S(2)}, u32[]{:S(2)}) async-start(bf16[96,32,128]{2,1,0:T(8,128)(2,1)} %bitcast.6), calls=%async_computation.1 | async-start | bytes 1572864 | tf_op jit(solution)/shard_map/all_to_all | solution.py:36
  60.2 4.2 %copy-start.4 = (bf16[4,32,3072]{2,1,0:T(8,128)(2,1)S(1)}, bf16[4,32,3072]{2,1,0:T(8,128)(2,1)}, u32[]{:S(2)}) copy-start(bf16[4,32,3072]{2,1,0:T(8,128)(2,1)} %param.12) | copy-start | bytes 2359300
  60.5 70.9 %collective-permute-start = (bf16[2,3,1024,128]{3,2,1,0:T(8,128)(2,1)S(1)}, bf16[2,3,1024,128]{3,2,1,0:T(8,128)(2,1)}, u32[]{:S(2)}, u32[]{:S(2)}) collective-permute-start(bf16[2,3,1024,128]{3,2,1,0:T(8,128)(2,1)S(1)} %get-tuple-element.112), channel_id=1, source_target_pairs={{0,8},{1,9},{2,10},{3,11},{4,12},{5,13},{6,14},{7,15},{8,16},{9,17... | collective-permute-start | bytes 4718600 | tf_op jit(solution)/shard_map/ppermute | solution.py:17
  64.5 115.9 %copy-start.7 = (s32[4]{0:T(128)S(1)}, s32[4]{0:T(128)}, u32[]{:S(2)}) copy-start(s32[4]{0:T(128)} %param.16) | copy-start | bytes 52
  131.4 93.3 %collective-permute-start.1 = (bf16[2,3,1024,128]{3,2,1,0:T(8,128)(2,1)}, bf16[2,3,1024,128]{3,2,1,0:T(8,128)(2,1)}, u32[]{:S(2)}, u32[]{:S(2)}) collective-permute-start(bf16[2,3,1024,128]{3,2,1,0:T(8,128)(2,1)} %collective-permute-done), channel_id=1, source_target_pairs={{0,8},{1,9},{2,10},{3,11},{4,12},{5,13},{6,14},{7,15},{8,16},{9,17... | collective-permute-start | bytes 4718600 | tf_op jit(solution)/shard_map/ppermute | solution.py:17
  135.3 89.4 %all-to-all-start = ((bf16[96,32,128]{2,1,0:T(8,128)(2,1)}), bf16[96,32,128]{2,1,0:T(8,128)(2,1)S(1)}, u32[]{:S(2)}, u32[]{:S(2)}) async-start(bf16[96,32,128]{2,1,0:T(8,128)(2,1)} %bitcast.1), calls=%async_computation | async-start | bytes 1572864 | tf_op jit(solution)/shard_map/all_to_all | solution.py:35
  226.9 2.5 copy-start.2
  297.3 10.9 %copy-start.8 = (s32[4]{0:T(128)S(1)}, s32[4]{0:T(128)}, u32[]{:S(2)}) copy-start(s32[4]{0:T(128)} %param.15) | copy-start | bytes 52
  297.3 10.9 %copy-start.9 = (f32[8]{0:T(128)S(1)}, f32[8]{0:T(128)}, u32[]{:S(2)}) copy-start(f32[8]{0:T(128)} %param.18) | copy-start | bytes 100
  299.0 35.5 %all-to-all-start.3 = ((bf16[3,1024,128]{2,0,1:T(4,128)(2,1)}), bf16[3,1024,128]{2,0,1:T(4,128)(2,1)S(1)}, u32[]{:S(2)}, u32[]{:S(2)}) async-start(bf16[3,1024,128]{2,0,1:T(4,128)(2,1)} %copy.60), calls=%async_computation.3 | async-start | bytes 2097152 | tf_op jit(solution)/shard_map/all_to_all | solution.py:79
  334.6 1.1 copy-start.5
  334.9 11.3 %copy-start.6 = (bf16[32,3072]{1,0:T(8,128)(2,1)S(1)}, bf16[32,3072]{1,0:T(8,128)(2,1)}, u32[]{:S(2)}) copy-start(bf16[32,3072]{1,0:T(8,128)(2,1)} %param.19) | copy-start | bytes 589828
  335.9 11.3 %copy-start.1 = (bf16[4,32,3072]{2,1,0:T(8,128)(2,1)}, bf16[4,32,3072]{2,1,0:T(8,128)(2,1)S(1)}, u32[]{:S(2)}) copy-start(bf16[4,32,3072]{2,1,0:T(8,128)(2,1)S(1)} %fusion.32) | copy-start | bytes 2359300
  335.9 10.2 %collective-permute-start.2 = (bf16[1,32,3072]{2,1,0:T(8,128)(2,1)S(1)}, bf16[1,32,3072]{2,1,0:T(8,128)(2,1)S(1)}, u32[]{:S(2)}, u32[]{:S(2)}) collective-permute-start(bf16[1,32,3072]{2,1,0:T(8,128)(2,1)S(1)} %slice.23), channel_id=1, source_target_pairs={{32,0},{64,32},{96,64},{128,96},{160,128},{192,160},{224,192},{256... | collective-permute-start | bytes 589832 | tf_op jit(solution)/shard_map/ppermute | solution.py:17
where the time goes:
time: 348 us; the launch traced here: 347 us
  waiting for transfers between devices  181 us (52%)
  starting transfers between devices  81.8 us (24%)
  local copies, waits for them, and re-layouts  30.5 us (9%)
  loops' own time  23.5 us (7%)
  matrix products  15.9 us (5%)
  other arithmetic  13.1 us (4%)
    ppermute x3, waiting for transfers between devices, from_behind(): lax.ppermute(value, axis, [(source, source + steps) for source in range(l...  72.4 us
    all_to_all x1, starting transfers between devices, per_device(): lax.all_to_all(split_heads(queries), 'tok', split_axis=0, concat_axis=1,...  45 us
    all_to_all x1, waiting for transfers between devices, per_device(): lax.all_to_all(split_heads(queries), 'tok', split_axis=0, concat_axis=1,...  43.1 us
    all_to_all x1, waiting for transfers between devices, per_device(): lax.all_to_all(attn_heads, 'tok', split_axis=1, concat_axis=0, tiled=True)  25.9 us
    another operation x1, loops' own time, per_device(): lax.map(one_block, jnp.arange(heads_here * blocks, dtype=jnp.int32))  23.5 us
    all_to_all x1, waiting for transfers between devices, per_device(): lax.all_to_all(split_heads(values), 'tok', split_axis=0, concat_axis=1, t...  19.8 us
    all_to_all x1, waiting for transfers between devices, per_device(): lax.all_to_all(split_heads(keys), 'tok', split_axis=0, concat_axis=1, til...  19.7 us
    slice x6, local copies, waits for them, and re-layouts, one_block(): value_rows = lax.dynamic_index_in_dim(window[1], head, 0, keepdims=False)  16.1 us
  transfers between devices with their start and end apart: 7, of which 6 were waited for; matrix products, arithmetic and copies ran while one was open for 1% of the time, Pallas kernels for 0%

commit v1 on v0

v1 whole, which is shorter than its diff:
```python
import functools
import math

import jax
import jax.numpy as jnp
from jax import lax
from jax.experimental import pallas as pl
from jax.experimental.pallas import tpu as pltpu
from jax.sharding import PartitionSpec as P

HEAD_DIM = 128
REACH = 2
FRAMES_HERE = 4
ROWS = 32
RING_Y = 8
RING_X = 4
GROUPS = 16
HEADS_HERE = 3
BLOCK = ROWS * RING_Y
FRAME_LEN = BLOCK * RING_X
WIDTH = RING_Y * HEADS_HERE * HEAD_DIM
SCALE = math.log2(math.e) / math.sqrt(HEAD_DIM)
MASKED = -1e30
MESH = pl.DeviceIdType.MESH
K, V, Q = 0, 1, 2
Y_STEPS = (4, 3, 5, 2, 6, 1, 7)
Y_ORDER = ((K, 0), (V, 0), (K, 1), (Q, 0), (V, 1), (K, 2), (Q, 1), (V, 2), (Q, 2))
K_RIGHT, K_LEFT, V_RIGHT, V_LEFT, K_RELAY, V_RELAY = range(6)
OWN, LEFT, RIGHT, FAR = range(4)


def kernel(
    latents, queries, keys, values, levels, reach, gates, steps_table, fresh,
    updated, next_queue,
    kbuf, vbuf, qbuf, obuf, attn, lat, gate, new, incoming,
    y_send, y_recv, y_here, x_send, x_recv, halo_send, halo_recv,
    o_send, o_recv, o_here, f_send, f_recv, in_sem,
):
    group = lax.axis_index("frame")
    place = lax.axis_index("tok")
    y, x = place // RING_X, place % RING_X
    bufs = {K: kbuf, V: vbuf, Q: qbuf}
    sources = {K: keys, V: values, Q: queries}

    def along_y(step):
        return (group, lax.rem(y + step, RING_Y) * RING_X + x)

    def along_x(step):
        return (group, y * RING_X + lax.rem(x + step + RING_X, RING_X))

    def along_frame(step):
        return (lax.rem(group + step + GROUPS, GROUPS), place)

    to_right, to_left = along_x(1), along_x(-1)
    next_group, last_group = along_frame(1), along_frame(-1)

    barrier = pltpu.get_barrier_semaphore()
    peers = [along_y(step) for step in range(1, RING_Y)] + [to_right, to_left, next_group, last_group]
    for peer in peers:
        pl.semaphore_signal(barrier, inc=1, device_id=peer, device_id_type=MESH)
    pl.semaphore_wait(barrier, len(peers))

    def columns(owner, head):
        return pl.ds(pl.multiple_of((owner * HEADS_HERE + head) * HEAD_DIM, HEAD_DIM), HEAD_DIM)

    def landing(array, head):
        rows = pl.multiple_of(y * ROWS, ROWS)
        if array == Q:
            return qbuf.at[head, :, pl.ds(rows, ROWS), :]
        rows = pl.multiple_of(x * BLOCK + y * ROWS, ROWS)
        return bufs[array].at[head, pl.ds(REACH, FRAMES_HERE), pl.ds(rows, ROWS), :]

    def y_copy(array, head, step):
        index = (array * HEADS_HERE + head) * RING_Y + step
        return pltpu.make_async_remote_copy(
            src_ref=sources[array].at[:, :, columns(lax.rem(y + step, RING_Y), head)],
            dst_ref=landing(array, head),
            send_sem=y_send.at[index],
            recv_sem=y_recv.at[index],
            device_id=along_y(step),
            device_id_type=MESH,
        )

    def y_own(array, head):
        return pltpu.make_async_copy(
            sources[array].at[:, :, columns(y, head)],
            landing(array, head),
            y_here.at[array * HEADS_HERE + head],
        )

    def block_rows(role):
        shift = {OWN: 0, LEFT: 3, RIGHT: 1, FAR: 2}[role]
        return pl.ds(pl.multiple_of(lax.rem(x + shift, RING_X) * BLOCK, BLOCK), BLOCK)

    def x_copy(head, kind):
        array = K if kind in (K_RIGHT, K_LEFT, K_RELAY) else V
        role = {K_RELAY: LEFT, V_RELAY: RIGHT}.get(kind, OWN)
        block = bufs[array].at[head, pl.ds(REACH, FRAMES_HERE), block_rows(role), :]
        return pltpu.make_async_remote_copy(
            src_ref=block,
            dst_ref=block,
            send_sem=x_send.at[head * 6 + kind],
            recv_sem=x_recv.at[head * 6 + kind],
            device_id=to_right if kind in (K_RIGHT, V_RIGHT, K_RELAY) else to_left,
            device_id_type=MESH,
        )

    def halo_copy(array, head, role):
        index = (array * HEADS_HERE + head) * 4 + role
        return pltpu.make_async_remote_copy(
            src_ref=bufs[array].at[head, pl.ds(FRAMES_HERE, REACH), block_rows(role), :],
            dst_ref=bufs[array].at[head, pl.ds(0, REACH), block_rows(role), :],
            send_sem=halo_send.at[index],
            recv_sem=halo_recv.at[index],
            device_id=next_group,
            device_id_type=MESH,
        )

    def o_copy(head, frame, step):
        index = (head * FRAMES_HERE + frame) * RING_Y + step
        rows = pl.ds(pl.multiple_of(lax.rem(y + step, RING_Y) * ROWS, ROWS), ROWS)
        return pltpu.make_async_remote_copy(
            src_ref=obuf.at[head, frame, rows, :],
            dst_ref=attn.at[frame, :, columns(y, head)],
            send_sem=o_send.at[index],
            recv_sem=o_recv.at[index],
            device_id=along_y(step),
            device_id_type=MESH,
        )

    def o_own(head, frame):
        rows = pl.ds(pl.multiple_of(y * ROWS, ROWS), ROWS)
        return pltpu.make_async_copy(
            obuf.at[head, frame, rows, :],
            attn.at[frame, :, columns(y, head)],
            o_here.at[head * FRAMES_HERE + frame],
        )

    frame_copy = pltpu.make_async_remote_copy(
        src_ref=new,
        dst_ref=incoming,
        send_sem=f_send.at[0],
        recv_sem=f_recv.at[0],
        device_id=last_group,
        device_id_type=MESH,
    )

    for array, head in Y_ORDER:
        for step in Y_STEPS:
            y_copy(array, head, step).start()
        y_own(array, head).start()
    lat_copy = pltpu.make_async_copy(latents, lat, in_sem.at[0])
    gate_copy = pltpu.make_async_copy(gates, gate, in_sem.at[1])
    lat_copy.start()
    gate_copy.start()

    def arrive(array, head):
        for step in Y_STEPS:
            y_copy(array, head, step).wait_recv()
        y_own(array, head).wait()

    def first(array, head):
        arrive(array, head)
        x_copy(head, K_RIGHT if array == K else V_RIGHT).start()
        x_copy(head, K_LEFT if array == K else V_LEFT).start()
        halo_copy(array, head, OWN).start()

    def second(array, head):
        from_left, from_right = (K_RIGHT, K_LEFT) if array == K else (V_RIGHT, V_LEFT)
        x_copy(head, from_left).wait_recv()
        if array == K:
            x_copy(head, K_RELAY).start()
        x_copy(head, from_right).wait_recv()
        if array == V:
            x_copy(head, V_RELAY).start()
        halo_copy(array, head, LEFT).start()
        halo_copy(array, head, RIGHT).start()

    def third(array, head):
        x_copy(head, K_RELAY if array == K else V_RELAY).wait_recv()
        halo_copy(array, head, FAR).start()

    def halo(head):
        for array in (K, V):
            for role in (OWN, LEFT, RIGHT, FAR):
                halo_copy(array, head, role).wait_recv()

    ones = jnp.ones((BLOCK, HEAD_DIM), jnp.bfloat16)

    def attend(head, frame):
        query = qbuf[head, frame]
        allowed_back = reach[frame]
        top = total = None
        for back in range(REACH + 1):
            if back:
                ok = (allowed_back >= back) & (group * FRAMES_HERE + frame >= back)
                bias = jnp.where(ok, jnp.float32(0), jnp.float32(MASKED))
            for part in range(RING_X):
                rows = pl.ds(part * BLOCK, BLOCK)
                scores = lax.dot_general(
                    query, kbuf[head, frame + REACH - back, rows, :], (((1,), (1,)), ((), ())),
                    preferred_element_type=jnp.float32,
                ) * SCALE
                best = jnp.max(scores, axis=1, keepdims=True)
                if back:
                    best = best + bias
                higher = best if top is None else jnp.maximum(top, best)
                weights = jnp.exp2(scores + (bias - higher if back else -higher))
                both = jnp.concatenate([vbuf[head, frame + REACH - back, rows, :], ones], 1)
                product = jnp.dot(weights.astype(jnp.bfloat16), both, preferred_element_type=jnp.float32)
                total = product if top is None else total * jnp.exp2(top - higher) + product
                top = higher
        obuf[head, frame] = (total[:, :HEAD_DIM] / total[:, HEAD_DIM:]).astype(jnp.bfloat16)

    def compute(head, start):
        def body(frame, carry):
            attend(head, frame)
            for step in Y_STEPS:
                o_copy(head, frame, step).start()
            o_own(head, frame).start()
            return carry

        lax.fori_loop(start, start + 2, body, 0)

    def finish(head):
        def waits(frame, carry):
            for step in Y_STEPS:
                o_copy(head, frame, step).wait_recv()
            o_own(head, frame).wait()
            return carry

        lax.fori_loop(0, FRAMES_HERE, waits, 0)
        for frame in range(FRAMES_HERE):
            level = levels[frame] - group * (2 * FRAMES_HERE)
            for owner in range(RING_Y):
                cols = pl.ds((owner * HEADS_HERE + head) * HEAD_DIM, HEAD_DIM)
                pair = gate[pl.ds(2 * frame, 2), cols].astype(jnp.float32)
                low, high = 2 * frame, 2 * frame + 1
                factor = jnp.where(level == low, steps_table[low] * pair[0:1], steps_table[high] * pair[1:2])
                result = lat[frame, :, cols].astype(jnp.float32) - factor * attn[frame, :, cols].astype(jnp.float32)
                result = result.astype(jnp.bfloat16)
                updated[frame, :, cols] = result
                if frame == 0:
                    new[:, cols] = result
                else:
                    next_queue[frame - 1, :, cols] = result

    first(K, 0)
    first(V, 0)
    second(K, 0)
    second(V, 0)
    first(K, 1)
    third(K, 0)
    third(V, 0)
    arrive(Q, 0)
    compute(0, 2)
    first(V, 1)
    second(K, 1)
    halo(0)
    compute(0, 0)
    second(V, 1)
    third(K, 1)
    first(K, 2)
    third(V, 1)
    arrive(Q, 1)
    compute(1, 2)
    second(K, 2)
    first(V, 2)
    halo(1)
    compute(1, 0)
    third(K, 2)
    lat_copy.wait()
    gate_copy.wait()
    finish(0)
    second(V, 2)
    third(V, 2)
    arrive(Q, 2)
    compute(2, 2)
    finish(1)
    halo(2)
    compute(2, 0)
    finish(2)
    frame_copy.start()
    frame_copy.wait_recv()

    is_last = group == GROUPS - 1

    @pl.when(is_last)
    def _():
        copy = pltpu.make_async_copy(fresh, next_queue.at[FRAMES_HERE - 1], in_sem.at[2])
        copy.start()
        copy.wait()

    @pl.when(jnp.logical_not(is_last))
    def _():
        next_queue[FRAMES_HERE - 1] = incoming[...]

    frame_copy.wait_send()
    for array, head in Y_ORDER:
        for step in Y_STEPS:
            y_copy(array, head, step).wait_send()
    for head in range(HEADS_HERE):
        for kind in range(6):
            x_copy(head, kind).wait_send()
        for array in (K, V):
            for role in (OWN, LEFT, RIGHT, FAR):
                halo_copy(array, head, role).wait_send()

        def drain(frame, carry):
            for step in Y_STEPS:
                o_copy(head, frame, step).wait_send()
            return carry

        lax.fori_loop(0, FRAMES_HERE, drain, 0)


def per_device(latents, queries, keys, values, levels, reach, gates, steps_table, fresh):
    shape = (FRAMES_HERE, ROWS, WIDTH)
    bf16 = jnp.bfloat16
    anywhere = pl.BlockSpec(memory_space=pl.ANY)
    scalars = pl.BlockSpec(memory_space=pltpu.SMEM)
    vmem = pl.BlockSpec(memory_space=pltpu.VMEM)
    dma = pltpu.SemaphoreType.DMA
    exchanged = 3 * HEADS_HERE * RING_Y
    window = (HEADS_HERE, FRAMES_HERE + REACH, FRAME_LEN, HEAD_DIM)
    mine = (HEADS_HERE, FRAMES_HERE, BLOCK, HEAD_DIM)
    return pl.pallas_call(
        kernel,
        out_shape=(jax.ShapeDtypeStruct(shape, bf16), jax.ShapeDtypeStruct(shape, bf16)),
        in_specs=[anywhere] * 4 + [scalars, scalars, anywhere, scalars, anywhere],
        out_specs=(vmem, vmem),
        scratch_shapes=[
            pltpu.VMEM(window, bf16),
            pltpu.VMEM(window, bf16),
            pltpu.VMEM(mine, bf16),
            pltpu.VMEM(mine, bf16),
            pltpu.VMEM(shape, bf16),
            pltpu.VMEM(shape, bf16),
            pltpu.VMEM((2 * FRAMES_HERE, WIDTH), bf16),
            pltpu.VMEM((ROWS, WIDTH), bf16),
            pltpu.VMEM((ROWS, WIDTH), bf16),
            dma((exchanged,)),
            dma((exchanged,)),
            dma((3 * HEADS_HERE,)),
            dma((6 * HEADS_HERE,)),
            dma((6 * HEADS_HERE,)),
            dma((8 * HEADS_HERE,)),
            dma((8 * HEADS_HERE,)),
            dma((HEADS_HERE * FRAMES_HERE * RING_Y,)),
            dma((HEADS_HERE * FRAMES_HERE * RING_Y,)),
            dma((HEADS_HERE * FRAMES_HERE,)),
            dma((1,)),
            dma((1,)),
            dma((3,)),
        ],
        compiler_params=pltpu.CompilerParams(
            collective_id=0, has_side_effects=True, vmem_limit_bytes=48 * 1024 * 1024
        ),
        cost_estimate=pl.CostEstimate(
            flops=9_700_000_000, bytes_accessed=8_000_000, transcendentals=9_500_000
        ),
    )(latents, queries, keys, values, levels, reach, gates, steps_table, fresh)


def solution(mesh):
    in_specs = (
        P("frame", "tok", None),
        P("frame", "tok", None),
        P("frame", "tok", None),
        P("frame", "tok", None),
        P("frame"),
        P("frame"),
        P("frame", None),
        P("frame"),
        P("tok", None),
    )
    out_specs = (P("frame", "tok", None), P("frame", "tok", None))
    return jax.shard_map(
        per_device, mesh=mesh, in_specs=in_specs, out_specs=out_specs, check_vma=False
    )
```

time: 348 us -> 112 us (0.32)
  the two profiles are of different devices: /device:TPU:1 before, /device:TPU:131 now
where the time goes in v1:
time: 112 us
  Pallas kernels  101 us (90%)
  local copies, waits for them, and re-layouts  9.97 us (9%)
    pallas_call x1, Pallas kernels, per_device(): pl.pallas_call(kernel, out_shape=(jax.ShapeDtypeStruct(shape, bf16), jax....  101 us
    unnamed x20, local copies, waits for them, and re-layouts  9.97 us

profile of v1, /device:TPU:131, one launch (start us, length us, event | category | flops | bytes accessed | tf_op | source)
XLA Modules:
  0.0 111.6 jit_solution(11784549010302191739)
XLA Ops:
  0.6 0.0 copy-start
  0.6 1.1 %copy-done = bf16[4,32,3072]{2,1,0:T(8,128)(2,1)S(1)} copy-done((bf16[4,32,3072]{2,1,0:T(8,128)(2,1)S(1)}, bf16[4,32,3072]{2,1,0:T(8,128)(2,1)}, u32[]{:S(2)}) %copy-start) | copy-done | bytes 786456
  1.8 0.0 copy-start.1
  1.8 1.1 %copy-done.1 = bf16[4,32,3072]{2,1,0:T(8,128)(2,1)S(1)} copy-done((bf16[4,32,3072]{2,1,0:T(8,128)(2,1)S(1)}, bf16[4,32,3072]{2,1,0:T(8,128)(2,1)}, u32[]{:S(2)}) %copy-start.1) | copy-done | bytes 786456
  2.9 0.0 copy-start.2
  2.9 1.1 %copy-done.2 = bf16[4,32,3072]{2,1,0:T(8,128)(2,1)S(1)} copy-done((bf16[4,32,3072]{2,1,0:T(8,128)(2,1)S(1)}, bf16[4,32,3072]{2,1,0:T(8,128)(2,1)}, u32[]{:S(2)}) %copy-start.2) | copy-done | bytes 786456
  4.0 0.0 copy-start.3
  4.0 1.1 %copy-done.3 = bf16[4,32,3072]{2,1,0:T(8,128)(2,1)S(1)} copy-done((bf16[4,32,3072]{2,1,0:T(8,128)(2,1)S(1)}, bf16[4,32,3072]{2,1,0:T(8,128)(2,1)}, u32[]{:S(2)}) %copy-start.3) | copy-done | bytes 786456
  5.2 0.0 copy-start.4
  5.2 0.9 copy-done.4
  6.1 0.0 copy-start.5
  6.1 0.8 copy-done.5
  6.9 0.0 copy-start.6
  6.9 0.7 copy-done.6
  7.6 0.0 copy-start.7
  7.6 0.7 copy-done.7
  8.2 0.0 copy-start.8
  8.2 0.7 copy-done.8
  8.9 100.9 %shard_map.104 = (bf16[4,32,3072]{2,1,0:T(8,128)(2,1)S(1)}, bf16[4,32,3072]{2,1,0:T(8,128)(2,1)S(1)}) custom-call(bf16[4,32,3072]{2,1,0:T(8,128)(2,1)S(1)} %copy-done, bf16[4,32,3072]{2,1,0:T(8,128)(2,1)S(1)} %copy-done.1, bf16[4,32,3072]{2,1,0:T(8,128)(2,1)S(1)} %copy-done.2, bf16[4,32,3072]{2,1,0:T(8,128)(2,1)S(1)} %copy-done.3, s32[4]{0:T(128)S(1)} %copy-done.6, ...), custom_call_target="tpu_custom_call" | custom-call | flops 9699999744 | bytes 8000000 | tf_op jit(solution)/shard_map/pallas_call | solution.py:327
  109.8 0.9 copy.13
  110.7 0.9 copy.14
Async XLA Ops:
  0.6 1.1 %copy-start = (bf16[4,32,3072]{2,1,0:T(8,128)(2,1)S(1)}, bf16[4,32,3072]{2,1,0:T(8,128)(2,1)}, u32[]{:S(2)}) copy-start(bf16[4,32,3072]{2,1,0:T(8,128)(2,1)} %latents.1) | copy-start | bytes 2359300
  1.8 1.1 %copy-start.1 = (bf16[4,32,3072]{2,1,0:T(8,128)(2,1)S(1)}, bf16[4,32,3072]{2,1,0:T(8,128)(2,1)}, u32[]{:S(2)}) copy-start(bf16[4,32,3072]{2,1,0:T(8,128)(2,1)} %queries.1) | copy-start | bytes 2359300
  2.9 1.1 %copy-start.2 = (bf16[4,32,3072]{2,1,0:T(8,128)(2,1)S(1)}, bf16[4,32,3072]{2,1,0:T(8,128)(2,1)}, u32[]{:S(2)}) copy-start(bf16[4,32,3072]{2,1,0:T(8,128)(2,1)} %keys.1) | copy-start | bytes 2359300
  4.0 1.1 %copy-start.3 = (bf16[4,32,3072]{2,1,0:T(8,128)(2,1)S(1)}, bf16[4,32,3072]{2,1,0:T(8,128)(2,1)}, u32[]{:S(2)}) copy-start(bf16[4,32,3072]{2,1,0:T(8,128)(2,1)} %values.1) | copy-start | bytes 2359300
  5.2 0.9 copy-start.4
  6.1 0.8 copy-start.5
  6.9 0.7 copy-start.6
  7.6 0.7 copy-start.7
  8.2 0.7 copy-start.8

commit v2 on v1

v2 whole, which is shorter than its diff:
```python
import math

import jax
import jax.numpy as jnp
from jax import lax
from jax.experimental import pallas as pl
from jax.experimental.pallas import tpu as pltpu
from jax.sharding import PartitionSpec as P

HEAD_DIM = 128
REACH = 2
FRAMES_HERE = 4
ROWS = 32
RING_Y = 8
RING_X = 4
GROUPS = 16
HEADS_HERE = 3
BLOCK = ROWS * RING_Y
FRAME_LEN = BLOCK * RING_X
WIDTH = RING_Y * HEADS_HERE * HEAD_DIM
PART = RING_Y * HEAD_DIM
SCALE = math.log2(math.e) / math.sqrt(HEAD_DIM)
MASKED = -1e30
MESH = pl.DeviceIdType.MESH
K, V, Q = 0, 1, 2
Y_STEPS = (4, 3, 5, 2, 6, 1, 7)
WHOLE, EARLY, LATE = (0, 4), (0, 2), (2, 2)
TO_RIGHT, TO_LEFT, RELAY_RIGHT, RELAY_LEFT = range(4)
OWN, LEFT, RIGHT, FAR = range(4)
NEAR = (OWN, LEFT, RIGHT)
ALL = (OWN, LEFT, RIGHT, FAR)
SPLIT = ((K, 0), (V, 2))


def pieces(array, head):
    return (LATE, EARLY) if (array, head) in SPLIT else (WHOLE,)


def kernel(
    latents, queries, keys, values, levels, reach, gates, steps_table, fresh,
    updated, next_queue,
    kbuf, vbuf, qbuf, obuf, attn, lat, gate, newest, new, incoming, totals, tops,
    level, window, step_size,
    y_send, y_recv, x_send, x_recv, halo_send, halo_recv,
    o_send, o_recv, f_send, f_recv, in_sem,
):
    group = lax.axis_index("frame")
    place = lax.axis_index("tok")
    y, x = place // RING_X, place % RING_X
    bufs = {K: kbuf, V: vbuf, Q: qbuf}
    sources = {K: keys, V: values, Q: queries}

    def along_y(step):
        return (group, lax.rem(y + step, RING_Y) * RING_X + x)

    def along_x(step):
        return (group, y * RING_X + lax.rem(x + step + RING_X, RING_X))

    def along_frame(step):
        return (lax.rem(group + step + GROUPS, GROUPS), place)

    to_right, to_left = along_x(1), along_x(-1)
    next_group, last_group = along_frame(1), along_frame(-1)

    local = [
        pltpu.make_async_copy(source, target, in_sem.at[index])
        for index, (source, target) in enumerate(
            ((levels, level), (reach, window), (steps_table, step_size), (gates, gate), (latents, lat), (fresh, newest))
        )
    ]

    barrier = pltpu.get_barrier_semaphore()
    peers = [along_y(step) for step in range(1, RING_Y)] + [to_right, to_left, next_group, last_group]
    for peer in peers:
        pl.semaphore_signal(barrier, inc=1, device_id=peer, device_id_type=MESH)
    pl.semaphore_wait(barrier, len(peers))

    def wait(ref, sem):
        pltpu.make_async_copy(ref, ref, sem).wait()

    def columns(owner, head):
        return pl.ds(pl.multiple_of((owner * HEADS_HERE + head) * HEAD_DIM, HEAD_DIM), HEAD_DIM)

    def block_rows(role):
        shift = {OWN: 0, LEFT: 3, RIGHT: 1, FAR: 2}[role]
        return pl.ds(pl.multiple_of(lax.rem(x + shift, RING_X) * BLOCK, BLOCK), BLOCK)

    def unit(array, head, piece):
        return (array * HEADS_HERE + head) * 2 + (piece == EARLY)

    def landing(array, head, piece):
        if array == Q:
            rows = pl.ds(pl.multiple_of(y * ROWS, ROWS), ROWS)
            return qbuf.at[head, pl.ds(*piece), rows, :]
        rows = pl.ds(pl.multiple_of(x * BLOCK + y * ROWS, ROWS), ROWS)
        return bufs[array].at[head, pl.ds(REACH + piece[0], piece[1]), rows, :]

    def y_copy(array, head, piece, step):
        owner = lax.rem(y + step, RING_Y)
        return pltpu.make_async_remote_copy(
            src_ref=sources[array].at[pl.ds(*piece), :, columns(owner, head)],
            dst_ref=landing(array, head, piece),
            send_sem=y_send.at[array * HEADS_HERE + head],
            recv_sem=y_recv.at[unit(array, head, piece)],
            device_id=along_y(step),
            device_id_type=MESH,
        )

    def exchange(array, head):
        for piece in pieces(array, head):
            for step in Y_STEPS:
                y_copy(array, head, piece, step).start()
            pltpu.make_async_copy(
                sources[array].at[pl.ds(*piece), :, columns(y, head)],
                landing(array, head, piece),
                y_recv.at[unit(array, head, piece)],
            ).start()

    def arrive(array, head, piece=WHOLE):
        if array == Q:
            block = qbuf.at[head, pl.ds(*piece)]
        else:
            block = bufs[array].at[head, pl.ds(REACH + piece[0], piece[1]), block_rows(OWN), :]
        wait(block, y_recv.at[unit(array, head, piece)])

    def x_copy(array, head, piece, kind):
        role = {RELAY_RIGHT: LEFT, RELAY_LEFT: RIGHT}.get(kind, OWN)
        first, count = piece
        if kind in (RELAY_RIGHT, RELAY_LEFT):
            count = count // 2
        if kind == RELAY_LEFT:
            first = first + count
        block = bufs[array].at[head, pl.ds(REACH + first, count), block_rows(role), :]
        return pltpu.make_async_remote_copy(
            src_ref=block,
            dst_ref=block,
            send_sem=x_send.at[array * HEADS_HERE + head],
            recv_sem=x_recv.at[unit(array, head, piece) * 4 + kind],
            device_id=to_right if kind in (TO_RIGHT, RELAY_RIGHT) else to_left,
            device_id_type=MESH,
        )

    def halo_index(array, head, far):
        return (array * HEADS_HERE + head) * 2 + far

    def halo_start(array, head, piece, role):
        if piece == EARLY:
            return
        pltpu.make_async_remote_copy(
            src_ref=bufs[array].at[head, pl.ds(FRAMES_HERE, REACH), block_rows(role), :],
            dst_ref=bufs[array].at[head, pl.ds(0, REACH), block_rows(role), :],
            send_sem=halo_send.at[array * HEADS_HERE + head],
            recv_sem=halo_recv.at[halo_index(array, head, role == FAR)],
            device_id=next_group,
            device_id_type=MESH,
        ).start()

    def halo(head, far):
        for array in (K, V):
            rows = pl.ds(0, BLOCK if far else 3 * BLOCK)
            wait(bufs[array].at[head, pl.ds(0, REACH), rows, :], halo_recv.at[halo_index(array, head, far)])

    def first(array, head, piece=WHOLE):
        arrive(array, head, piece)
        x_copy(array, head, piece, TO_RIGHT).start()
        x_copy(array, head, piece, TO_LEFT).start()
        halo_start(array, head, piece, OWN)

    def second(array, head, piece=WHOLE):
        x_copy(array, head, piece, TO_RIGHT).wait_recv()
        x_copy(array, head, piece, RELAY_RIGHT).start()
        x_copy(array, head, piece, TO_LEFT).wait_recv()
        x_copy(array, head, piece, RELAY_LEFT).start()
        halo_start(array, head, piece, LEFT)
        halo_start(array, head, piece, RIGHT)

    def third(array, head, piece=WHOLE):
        x_copy(array, head, piece, RELAY_RIGHT).wait_recv()
        x_copy(array, head, piece, RELAY_LEFT).wait_recv()
        halo_start(array, head, piece, FAR)

    ones = jnp.ones((BLOCK, HEAD_DIM), jnp.bfloat16)

    def attend(head, frame, roles, begin, end):
        query = qbuf[head, frame]
        allowed_back = window[frame]
        if begin:
            top = total = None
        else:
            top, total = tops[frame][:, :1], totals[frame]
        for back in range(REACH + 1):
            ok = (allowed_back >= back) & (group * FRAMES_HERE + frame >= back)
            bias = jnp.where(ok, jnp.float32(0), jnp.float32(MASKED))
            for role in roles:
                rows = block_rows(role)
                scores = lax.dot_general(
                    query, kbuf[head, frame + REACH - back, rows, :], (((1,), (1,)), ((), ())),
                    preferred_element_type=jnp.float32,
                ) * SCALE
                best = jnp.max(scores, axis=1, keepdims=True)
                if back:
                    best = best + bias
                higher = best if top is None else jnp.maximum(top, best)
                weights = jnp.exp2(scores + (bias - higher if back else -higher))
                both = jnp.concatenate([vbuf[head, frame + REACH - back, rows, :], ones], 1)
                product = jnp.dot(weights.astype(jnp.bfloat16), both, preferred_element_type=jnp.float32)
                total = product if top is None else total * jnp.exp2(top - higher) + product
                top = higher
        if end:
            obuf[head, frame] = (total[:, :HEAD_DIM] / total[:, HEAD_DIM:]).astype(jnp.bfloat16)
        else:
            tops[frame] = jnp.broadcast_to(top, (BLOCK, HEAD_DIM))
            totals[frame] = total

    def give_back(head, frame):
        for step in Y_STEPS:
            rows = pl.ds(pl.multiple_of(lax.rem(y + step, RING_Y) * ROWS, ROWS), ROWS)
            pltpu.make_async_remote_copy(
                src_ref=obuf.at[head, frame, rows, :],
                dst_ref=attn.at[frame, :, columns(y, head)],
                send_sem=o_send.at[head],
                recv_sem=o_recv.at[head * FRAMES_HERE + frame],
                device_id=along_y(step),
                device_id_type=MESH,
            ).start()
        rows = pl.ds(pl.multiple_of(y * ROWS, ROWS), ROWS)
        pltpu.make_async_copy(
            obuf.at[head, frame, rows, :],
            attn.at[frame, :, columns(y, head)],
            o_recv.at[head * FRAMES_HERE + frame],
        ).start()

    def compute(head, start, count, roles=ALL, begin=True, end=True):
        def body(frame, carry):
            attend(head, frame, roles, begin, end)
            if end:
                give_back(head, frame)
            return carry

        lax.fori_loop(start, start + count, body, 0)

    def frame_copy(head):
        return pltpu.make_async_remote_copy(
            src_ref=new.at[head],
            dst_ref=incoming.at[head],
            send_sem=f_send.at[head],
            recv_sem=f_recv.at[head],
            device_id=last_group,
            device_id_type=MESH,
        )

    def finish(head, start, count):
        for frame in range(start, start + count):
            wait(attn.at[frame, :, pl.ds(0, PART)], o_recv.at[head * FRAMES_HERE + frame])
            low, high = 2 * frame, 2 * frame + 1
            is_low = level[frame] == group * (2 * FRAMES_HERE) + low
            for owner in range(RING_Y):
                cols = pl.ds((owner * HEADS_HERE + head) * HEAD_DIM, HEAD_DIM)
                pair = gate[:, cols].astype(jnp.float32)
                factor = jnp.where(is_low, step_size[low] * pair[low:high], step_size[high] * pair[high:high + 1])
                result = lat[frame, :, cols].astype(jnp.float32) - factor * attn[frame, :, cols].astype(jnp.float32)
                result = result.astype(jnp.bfloat16)
                updated[frame, :, cols] = result
                if frame == 0:
                    new[head, :, pl.ds(owner * HEAD_DIM, HEAD_DIM)] = result
                else:
                    next_queue[frame - 1, :, cols] = result
            if frame == 0:
                frame_copy(head).start()

    is_last = group == GROUPS - 1

    def enter(head):
        frame_copy(head).wait_recv()
        for owner in range(RING_Y):
            cols = pl.ds((owner * HEADS_HERE + head) * HEAD_DIM, HEAD_DIM)
            came = incoming[head, :, pl.ds(owner * HEAD_DIM, HEAD_DIM)]
            next_queue[FRAMES_HERE - 1, :, cols] = jnp.where(is_last, newest[:, cols], came)

    def prepare():
        for copy in local:
            copy.start()

    def prepared():
        for copy in local:
            copy.wait()

    exchange(K, 0)
    exchange(V, 0)
    exchange(K, 1)
    exchange(Q, 0)
    exchange(V, 1)
    exchange(K, 2)
    exchange(Q, 1)
    exchange(V, 2)
    exchange(Q, 2)
    prepare()
    first(K, 0, LATE)
    first(K, 0, EARLY)
    first(V, 0)
    second(K, 0, LATE)
    second(K, 0, EARLY)
    prepared()
    second(V, 0)
    first(K, 1)
    third(K, 0, LATE)
    third(K, 0, EARLY)
    third(V, 0)
    arrive(Q, 0)
    compute(0, 2, 2)
    first(V, 1)
    second(K, 1)
    halo(0, False)
    halo(0, True)
    compute(0, 0, 2)
    second(V, 1)
    third(K, 1)
    first(K, 2)
    third(V, 1)
    arrive(Q, 1)
    compute(1, 2, 2)
    second(K, 2)
    first(V, 2, LATE)
    first(V, 2, EARLY)
    halo(1, False)
    halo(1, True)
    compute(1, 0, 2)
    third(K, 2)
    second(V, 2, LATE)
    second(V, 2, EARLY)
    arrive(Q, 2)
    third(V, 2, LATE)
    third(V, 2, EARLY)
    compute(2, 2, 2)
    halo(2, False)
    halo(2, True)
    compute(2, 0, 2)
    finish(0, 0, 4)
    finish(1, 0, 4)
    finish(2, 0, 1)
    finish(2, 1, 3)
    enter(0)
    enter(1)
    enter(2)

    away = BLOCK - ROWS
    for head in range(HEADS_HERE):
        frame_copy(head).wait_send()
        for array in (K, V, Q):
            wait(qbuf.at[head, :, pl.ds(0, away), :], y_send.at[array * HEADS_HERE + head])
        for array in (K, V):
            index = array * HEADS_HERE + head
            wait(bufs[array].at[head, pl.ds(0, FRAMES_HERE), pl.ds(0, 3 * BLOCK), :], x_send.at[index])
            wait(bufs[array].at[head, pl.ds(0, REACH)], halo_send.at[index])
        wait(obuf.at[head, :, pl.ds(0, away), :], o_send.at[head])


def per_device(latents, queries, keys, values, levels, reach, gates, steps_table, fresh):
    shape = (FRAMES_HERE, ROWS, WIDTH)
    bf16 = jnp.bfloat16
    hbm = pl.BlockSpec(memory_space=pltpu.HBM)
    vmem = pl.BlockSpec(memory_space=pltpu.VMEM)
    dma = pltpu.SemaphoreType.DMA
    span = (HEADS_HERE, FRAMES_HERE + REACH, FRAME_LEN, HEAD_DIM)
    mine = (HEADS_HERE, FRAMES_HERE, BLOCK, HEAD_DIM)
    return pl.pallas_call(
        kernel,
        out_shape=(jax.ShapeDtypeStruct(shape, bf16), jax.ShapeDtypeStruct(shape, bf16)),
        in_specs=[hbm] * 9,
        out_specs=(vmem, vmem),
        scratch_shapes=[
            pltpu.VMEM(span, bf16),
            pltpu.VMEM(span, bf16),
            pltpu.VMEM(mine, bf16),
            pltpu.VMEM(mine, bf16),
            pltpu.VMEM(shape, bf16),
            pltpu.VMEM(shape, bf16),
            pltpu.VMEM((2 * FRAMES_HERE, WIDTH), bf16),
            pltpu.VMEM((ROWS, WIDTH), bf16),
            pltpu.VMEM((HEADS_HERE, ROWS, PART), bf16),
            pltpu.VMEM((HEADS_HERE, ROWS, PART), bf16),
            pltpu.VMEM((FRAMES_HERE, BLOCK, 2 * HEAD_DIM), jnp.float32),
            pltpu.VMEM((FRAMES_HERE, BLOCK, HEAD_DIM), jnp.float32),
            pltpu.SMEM((FRAMES_HERE,), jnp.int32),
            pltpu.SMEM((FRAMES_HERE,), jnp.int32),
            pltpu.SMEM((2 * FRAMES_HERE,), jnp.float32),
            dma((3 * HEADS_HERE,)),
            dma((6 * HEADS_HERE,)),
            dma((2 * HEADS_HERE,)),
            dma((16 * HEADS_HERE,)),
            dma((2 * HEADS_HERE,)),
            dma((4 * HEADS_HERE,)),
            dma((HEADS_HERE,)),
            dma((HEADS_HERE * FRAMES_HERE,)),
            dma((HEADS_HERE,)),
            dma((HEADS_HERE,)),
            dma((6,)),
        ],
        compiler_params=pltpu.CompilerParams(
            collective_id=0, has_side_effects=True, vmem_limit_bytes=62 * 1024 * 1024
        ),
        cost_estimate=pl.CostEstimate(
            flops=9_700_000_000, bytes_accessed=8_000_000, transcendentals=9_500_000
        ),
    )(latents, queries, keys, values, levels, reach, gates, steps_table, fresh)


def solution(mesh):
    in_specs = (
        P("frame", "tok", None),
        P("frame", "tok", None),
        P("frame", "tok", None),
        P("frame", "tok", None),
        P("frame"),
        P("frame"),
        P("frame", None),
        P("frame"),
        P("tok", None),
    )
    out_specs = (P("frame", "tok", None), P("frame", "tok", None))
    return jax.shard_map(
        per_device, mesh=mesh, in_specs=in_specs, out_specs=out_specs, check_vma=False
    )
```

time: 112 us -> 92.1 us (0.82)
  the two profiles are of different devices: /device:TPU:131 before, /device:TPU:1 now
where the time goes in v2:
time: 92.1 us; the launch traced here: 91.9 us
  Pallas kernels  88.3 us (96%)
  local copies, waits for them, and re-layouts  3.02 us (3%)
    pallas_call x1, Pallas kernels, per_device(): pl.pallas_call(kernel, out_shape=(jax.ShapeDtypeStruct(shape, bf16), jax....  88.3 us
    unnamed x4, local copies, waits for them, and re-layouts  3.02 us

profile of v2, /device:TPU:1, one launch (start us, length us, event | category | flops | bytes accessed | tf_op | source)
XLA Modules:
  0.0 91.9 jit_solution(997401161772945794)
XLA Ops:
  0.6 88.3 %shard_map.104 = (bf16[4,32,3072]{2,1,0:T(8,128)(2,1)}, bf16[4,32,3072]{2,1,0:T(8,128)(2,1)}) custom-call(bf16[4,32,3072]{2,1,0:T(8,128)(2,1)} %latents.1, bf16[4,32,3072]{2,1,0:T(8,128)(2,1)} %queries.1, bf16[4,32,3072]{2,1,0:T(8,128)(2,1)} %keys.1, bf16[4,32,3072]{2,1,0:T(8,128)(2,1)} %values.1, s32[4]{0:T(128)} %levels.1, s32[4]{0:T(128)} %reach.1, ...), custom_call_target="tpu_custom_call" | custom-call | flops 9699999744 | bytes 8000000 | tf_op jit(solution)/shard_map/pallas_call | solution.py:366
  88.9 0.0 copy-start
  88.9 2.1 %copy.13 = bf16[4,32,3072]{2,1,0:T(8,128)(2,1)} copy(bf16[4,32,3072]{2,1,0:T(8,128)(2,1)} %get-tuple-element.4) | data formatting | bytes 1572864
  91.1 0.0 copy-done
  91.1 0.9 copy.14
Async XLA Ops:
  88.9 2.1 %copy-start = (bf16[4,32,3072]{2,1,0:T(8,128)(2,1)S(1)}, bf16[4,32,3072]{2,1,0:T(8,128)(2,1)}, u32[]{:S(2)}) copy-start(bf16[4,32,3072]{2,1,0:T(8,128)(2,1)} %get-tuple-element.5) | copy-start | bytes 2359300

commit v3 on v2

--- a/solution.py
+++ b/solution.py
@@ -29,7 +29,7 @@
 OWN, LEFT, RIGHT, FAR = range(4)
 NEAR = (OWN, LEFT, RIGHT)
 ALL = (OWN, LEFT, RIGHT, FAR)
-SPLIT = ((K, 0), (V, 2))
+SPLIT = tuple((a, h) for a in (K, V) for h in range(HEADS_HERE))
 
 
 def pieces(array, head):
@@ -297,50 +297,63 @@
     prepare()
     first(K, 0, LATE)
     first(K, 0, EARLY)
-    first(V, 0)
+    first(V, 0, LATE)
+    first(V, 0, EARLY)
     second(K, 0, LATE)
     second(K, 0, EARLY)
     prepared()
-    second(V, 0)
-    first(K, 1)
+    second(V, 0, LATE)
+    second(V, 0, EARLY)
+    first(K, 1, LATE)
+    first(K, 1, EARLY)
     third(K, 0, LATE)
     third(K, 0, EARLY)
-    third(V, 0)
+    third(V, 0, LATE)
+    third(V, 0, EARLY)
     arrive(Q, 0)
     compute(0, 2, 2)
-    first(V, 1)
-    second(K, 1)
+    first(V, 1, LATE)
+    first(V, 1, EARLY)
+    second(K, 1, LATE)
+    second(K, 1, EARLY)
     halo(0, False)
     halo(0, True)
     compute(0, 0, 2)
-    second(V, 1)
-    third(K, 1)
-    first(K, 2)
-    third(V, 1)
+    second(V, 1, LATE)
+    second(V, 1, EARLY)
+    third(K, 1, LATE)
+    third(K, 1, EARLY)
+    first(K, 2, LATE)
+    first(K, 2, EARLY)
+    third(V, 1, LATE)
+    third(V, 1, EARLY)
     arrive(Q, 1)
     compute(1, 2, 2)
-    second(K, 2)
+    second(K, 2, LATE)
+    second(K, 2, EARLY)
     first(V, 2, LATE)
     first(V, 2, EARLY)
     halo(1, False)
     halo(1, True)
     compute(1, 0, 2)
-    third(K, 2)
+    third(K, 2, LATE)
+    third(K, 2, EARLY)
     second(V, 2, LATE)
     second(V, 2, EARLY)
     arrive(Q, 2)
     third(V, 2, LATE)
     third(V, 2, EARLY)
-    compute(2, 2, 2)
+    compute(2, 2, 1)
     halo(2, False)
     halo(2, True)
     compute(2, 0, 2)
+    compute(2, 3, 1)
     finish(0, 0, 4)
     finish(1, 0, 4)
     finish(2, 0, 1)
-    finish(2, 1, 3)
     enter(0)
     enter(1)
+    finish(2, 1, 3)
     enter(2)
 
     away = BLOCK - ROWS

time: 92.1 us -> 87.9 us (0.954)
  Pallas kernels: 88.3 us -> 83.3 us
    pallas_call x1, Pallas kernels: 88.3 us -> 83.3 us  [per_device(): pl.pallas_call(kernel, out_shape=(jax.ShapeDtypeStruct(shape, bf16), jax....]
where the time goes in v3:
time: 87.9 us; the launch traced here: 87 us
  Pallas kernels  83.3 us (95%)
  local copies, waits for them, and re-layouts  3.02 us (3%)
    pallas_call x1, Pallas kernels, per_device(): pl.pallas_call(kernel, out_shape=(jax.ShapeDtypeStruct(shape, bf16), jax....  83.3 us
    unnamed x4, local copies, waits for them, and re-layouts  3.02 us

profile of v3, /device:TPU:1, one launch (start us, length us, event | category | flops | bytes accessed | tf_op | source)
XLA Modules:
  0.0 87.0 jit_solution(7068582407807330464)
XLA Ops:
  0.6 83.3 %shard_map.104 = (bf16[4,32,3072]{2,1,0:T(8,128)(2,1)}, bf16[4,32,3072]{2,1,0:T(8,128)(2,1)}) custom-call(bf16[4,32,3072]{2,1,0:T(8,128)(2,1)} %latents.1, bf16[4,32,3072]{2,1,0:T(8,128)(2,1)} %queries.1, bf16[4,32,3072]{2,1,0:T(8,128)(2,1)} %keys.1, bf16[4,32,3072]{2,1,0:T(8,128)(2,1)} %values.1, s32[4]{0:T(128)} %levels.1, s32[4]{0:T(128)} %reach.1, ...), custom_call_target="tpu_custom_call" | custom-call | flops 9699999744 | bytes 8000000 | tf_op jit(solution)/shard_map/pallas_call | solution.py:379
  84.0 0.0 copy-start
  84.0 2.1 %copy.13 = bf16[4,32,3072]{2,1,0:T(8,128)(2,1)} copy(bf16[4,32,3072]{2,1,0:T(8,128)(2,1)} %get-tuple-element.4) | data formatting | bytes 1572864
  86.1 0.0 copy-done
  86.1 0.9 %copy.14 = bf16[4,32,3072]{2,1,0:T(8,128)(2,1)} copy(bf16[4,32,3072]{2,1,0:T(8,128)(2,1)S(1)} %copy-done) | data formatting | bytes 1572864
Async XLA Ops:
  84.0 2.1 %copy-start = (bf16[4,32,3072]{2,1,0:T(8,128)(2,1)S(1)}, bf16[4,32,3072]{2,1,0:T(8,128)(2,1)}, u32[]{:S(2)}) copy-start(bf16[4,32,3072]{2,1,0:T(8,128)(2,1)} %get-tuple-element.5) | copy-start | bytes 2359300

commit v4 on v3

--- a/solution.py
+++ b/solution.py
@@ -37,9 +37,9 @@
 
 
 def kernel(
-    latents, queries, keys, values, levels, reach, gates, steps_table, fresh,
-    updated, next_queue,
-    kbuf, vbuf, qbuf, obuf, attn, lat, gate, newest, new, incoming, totals, tops,
+    latents, queries, keys, values, levels, reach, gates, steps_table,
+    attended, next_queue, factors,
+    kbuf, vbuf, qbuf, obuf, attn, lat, gate, new, incoming, totals, tops,
     level, window, step_size,
     y_send, y_recv, x_send, x_recv, halo_send, halo_recv,
     o_send, o_recv, f_send, f_recv, in_sem,
@@ -65,7 +65,7 @@
     local = [
         pltpu.make_async_copy(source, target, in_sem.at[index])
         for index, (source, target) in enumerate(
-            ((levels, level), (reach, window), (steps_table, step_size), (gates, gate), (latents, lat), (fresh, newest))
+            ((levels, level), (reach, window), (steps_table, step_size), (gates, gate), (latents, lat))
         )
     ]
 
@@ -260,7 +260,8 @@
                 factor = jnp.where(is_low, step_size[low] * pair[low:high], step_size[high] * pair[high:high + 1])
                 result = lat[frame, :, cols].astype(jnp.float32) - factor * attn[frame, :, cols].astype(jnp.float32)
                 result = result.astype(jnp.bfloat16)
-                updated[frame, :, cols] = result
+                attended[frame, :, cols] = attn[frame, :, cols]
+                factors[pl.ds(frame, 1), cols] = factor
                 if frame == 0:
                     new[head, :, pl.ds(owner * HEAD_DIM, HEAD_DIM)] = result
                 else:
@@ -268,14 +269,11 @@
             if frame == 0:
                 frame_copy(head).start()
 
-    is_last = group == GROUPS - 1
-
     def enter(head):
         frame_copy(head).wait_recv()
         for owner in range(RING_Y):
             cols = pl.ds((owner * HEADS_HERE + head) * HEAD_DIM, HEAD_DIM)
-            came = incoming[head, :, pl.ds(owner * HEAD_DIM, HEAD_DIM)]
-            next_queue[FRAMES_HERE - 1, :, cols] = jnp.where(is_last, newest[:, cols], came)
+            next_queue[FRAMES_HERE - 1, :, cols] = incoming[head, :, pl.ds(owner * HEAD_DIM, HEAD_DIM)]
 
     def prepare():
         for copy in local:
@@ -376,11 +374,15 @@
     dma = pltpu.SemaphoreType.DMA
     span = (HEADS_HERE, FRAMES_HERE + REACH, FRAME_LEN, HEAD_DIM)
     mine = (HEADS_HERE, FRAMES_HERE, BLOCK, HEAD_DIM)
-    return pl.pallas_call(
+    attended, queue, factors = pl.pallas_call(
         kernel,
-        out_shape=(jax.ShapeDtypeStruct(shape, bf16), jax.ShapeDtypeStruct(shape, bf16)),
-        in_specs=[hbm] * 9,
-        out_specs=(vmem, vmem),
+        out_shape=(
+            jax.ShapeDtypeStruct(shape, bf16),
+            jax.ShapeDtypeStruct(shape, bf16),
+            jax.ShapeDtypeStruct((FRAMES_HERE, WIDTH), jnp.float32),
+        ),
+        in_specs=[hbm] * 8,
+        out_specs=(vmem, vmem, vmem),
         scratch_shapes=[
             pltpu.VMEM(span, bf16),
             pltpu.VMEM(span, bf16),
@@ -389,7 +391,6 @@
             pltpu.VMEM(shape, bf16),
             pltpu.VMEM(shape, bf16),
             pltpu.VMEM((2 * FRAMES_HERE, WIDTH), bf16),
-            pltpu.VMEM((ROWS, WIDTH), bf16),
             pltpu.VMEM((HEADS_HERE, ROWS, PART), bf16),
             pltpu.VMEM((HEADS_HERE, ROWS, PART), bf16),
             pltpu.VMEM((FRAMES_HERE, BLOCK, 2 * HEAD_DIM), jnp.float32),
@@ -407,7 +408,7 @@
             dma((HEADS_HERE * FRAMES_HERE,)),
             dma((HEADS_HERE,)),
             dma((HEADS_HERE,)),
-            dma((6,)),
+            dma((5,)),
         ],
         compiler_params=pltpu.CompilerParams(
             collective_id=0, has_side_effects=True, vmem_limit_bytes=62 * 1024 * 1024
@@ -415,7 +416,11 @@
         cost_estimate=pl.CostEstimate(
             flops=9_700_000_000, bytes_accessed=8_000_000, transcendentals=9_500_000
         ),
-    )(latents, queries, keys, values, levels, reach, gates, steps_table, fresh)
+    )(latents, queries, keys, values, levels, reach, gates, steps_table)
+    updated = latents.astype(jnp.float32) - factors[:, None, :] * attended.astype(jnp.float32)
+    slot = jnp.arange(FRAMES_HERE, dtype=jnp.int32)[:, None, None]
+    is_fresh = (slot == FRAMES_HERE - 1) & (lax.axis_index("frame") == GROUPS - 1)
+    return updated.astype(bf16), jnp.where(is_fresh, fresh[None], queue)
 
 
 def solution(mesh):

time: 87.9 us -> 88.4 us (level)
  other arithmetic: 0 us -> 3.37 us
  local copies, waits for them, and re-layouts: 3.02 us -> 0.01 us
    unnamed x4 -> x6, local copies, waits for them, and re-layouts: 3.02 us -> 0.01 us
    convert_element_type x0 -> x1, other arithmetic: none -> 2.35 us  [per_device(): return (updated.astype(bf16), jnp.where(is_fresh, fresh[None], queue))]
    select_n x0 -> x1, other arithmetic: none -> 1.01 us  [per_device(): return (updated.astype(bf16), jnp.where(is_fresh, fresh[None], queue))]
where the time goes in v4:
time: 88.4 us; the launch traced here: 87.5 us
  Pallas kernels  83.4 us (94%)
  other arithmetic  3.37 us (4%)
    pallas_call x1, Pallas kernels, per_device(): pl.pallas_call(kernel, out_shape=(jax.ShapeDtypeStruct(shape, bf16), jax....  83.4 us
    convert_element_type x1, other arithmetic, per_device(): return (updated.astype(bf16), jnp.where(is_fresh, fresh[None], queue))  2.35 us

profile of v4, /device:TPU:1, one launch (start us, length us, event | category | flops | bytes accessed | tf_op | source)
XLA Modules:
  0.0 87.5 jit_solution(1170087948188759535)
XLA Ops:
  0.6 0.0 copy-start
  0.6 83.4 %shard_map.104 = (bf16[4,32,3072]{2,1,0:T(8,128)(2,1)}, bf16[4,32,3072]{2,1,0:T(8,128)(2,1)}, f32[4,3072]{1,0:T(4,128)}) custom-call(bf16[4,32,3072]{2,1,0:T(8,128)(2,1)} %latents.1, bf16[4,32,3072]{2,1,0:T(8,128)(2,1)} %queries.1, bf16[4,32,3072]{2,1,0:T(8,128)(2,1)} %keys.1, bf16[4,32,3072]{2,1,0:T(8,128)(2,1)} %values.1, s32[4]{0:T(128)} %levels.1, ...), custom_call_target="tpu_custom_call" | custom-call | flops 9699999744 | bytes 8000000 | tf_op jit(solution)/shard_map/pallas_call | solution.py:377
  84.1 0.0 copy-done
  84.1 0.0 copy-start.1
  84.1 0.0 copy-start.2
  84.1 2.4 %subtract_convert_fusion = bf16[4,32,3072]{2,1,0:T(8,128)(2,1)} fusion(bf16[4,32,3072]{2,1,0:T(8,128)(2,1)} %get-tuple-element.6, bf16[4,32,3072]{2,1,0:T(8,128)(2,1)S(1)} %copy-done, f32[4,3072]{1,0:T(4,128)} %get-tuple-element.5), kind=kLoop, calls=%fused_computation | loop fusion | flops 1966080 | bytes 2408448 | tf_op jit(solution)/shard_map/convert_element_type | solution.py:423
  86.5 0.0 copy-done.1
  86.5 0.0 copy-done.2
  86.5 1.0 %broadcast_select_fusion = bf16[4,32,3072]{2,1,0:T(8,128)(2,1)} fusion(bf16[4,32,3072]{2,1,0:T(8,128)(2,1)S(1)} %copy-done.1, pred[4]{0:T(512)(128)(4,1)S(1)} %compare_and_fusion, bf16[32,3072]{1,0:T(8,128)(2,1)S(1)} %copy-done.2), kind=kLoop, calls=%fused_computation.1 | loop fusion | flops 393216 | bytes 1769476 | tf_op jit(solution)/shard_map/jit(_where)/select_n | solution.py:423
  (1 shorter events, 0.0 us)
Async XLA Ops:
  0.6 83.5 %copy-start = (bf16[4,32,3072]{2,1,0:T(8,128)(2,1)S(1)}, bf16[4,32,3072]{2,1,0:T(8,128)(2,1)}, u32[]{:S(2)}) copy-start(bf16[4,32,3072]{2,1,0:T(8,128)(2,1)} %latents.1) | copy-start | bytes 2359300
  84.1 2.4 %copy-start.1 = (bf16[4,32,3072]{2,1,0:T(8,128)(2,1)S(1)}, bf16[4,32,3072]{2,1,0:T(8,128)(2,1)}, u32[]{:S(2)}) copy-start(bf16[4,32,3072]{2,1,0:T(8,128)(2,1)} %get-tuple-element.7) | copy-start | bytes 2359300
  84.1 2.4 %copy-start.2 = (bf16[32,3072]{1,0:T(8,128)(2,1)S(1)}, bf16[32,3072]{1,0:T(8,128)(2,1)}, u32[]{:S(2)}) copy-start(bf16[32,3072]{1,0:T(8,128)(2,1)} %param.17) | copy-start | bytes 589828
